TPU v7x, 128 devices: a whole 4x4x4 slice. The times are simulated.
128 devices in a mesh: fsdp: 16 (over x, y_hi, core), node: 8 (over y_lo, z).
Axes of the slice: x: 4, y: 4 (y_hi: 2, y_lo: 2; y = y_hi * 2 + y_lo), z: 4, core: 2. Of those that a mesh axis runs over, the one named last changes fastest.
Arguments:
- activations: bfloat16 [8192, 8192], P('fsdp', 'node'), may hold values from -6 to 6
- qkv_weight: bfloat16 [8192, 5120], P('fsdp', 'node'), may hold values from -0.09375 to 0.09375
- qkv_grad: bfloat16 [8192, 5120], P('fsdp', 'node'), may hold values from -6 to 6
Outputs:
- projected: bfloat16 [8192, 5120], P('fsdp', 'node')
- input_grad: bfloat16 [8192, 8192], P('fsdp', 'node')
- weight_grad: float32 [8192, 5120], P('fsdp', 'node')
All inputs are finite; a program needn't handle non-finite values.
Results may differ from a plain program's by a relative error of at most 0.017.
Values may be sent and summed in bfloat16 or wider, within the bound.
No kernel may reach another device: no remote copies, remote signals or barrier semaphores. Data moves between devices by JAX's collectives and lax.ppermute only.
A program may use at most 128 MiB of HBM per device.

v0:
```python
import jax
import jax.numpy as jnp
from jax import lax
from jax.sharding import PartitionSpec as P


def body(activations, qkv_weight, qkv_grad):
    gathered = lax.all_gather(activations, "node", axis=1, tiled=True)
    feature_cols = gathered
    forward = jnp.dot(
        feature_cols,
        lax.all_gather(qkv_weight, "fsdp", axis=0, tiled=True),
        preferred_element_type=jnp.float32,
    )
    partial_sum = lax.dot_general(
        qkv_grad,
        lax.all_gather(qkv_weight, "fsdp", axis=0, tiled=True),
        (((1,), (1,)), ((), ())),
        preferred_element_type=jnp.float32,
    )
    projected = forward.astype(jnp.bfloat16)
    input_grad = lax.psum_scatter(
        partial_sum.astype(jnp.bfloat16), "node", scatter_dimension=1, tiled=True
    )
    feature_cols = gathered
    weight_grad = lax.psum_scatter(
        lax.dot_general(
            feature_cols, qkv_grad, (((0,), (0,)), ((), ())), preferred_element_type=jnp.float32
        ).astype(jnp.bfloat16),
        "fsdp",
        scatter_dimension=0,
        tiled=True,
    ).astype(jnp.float32)
    return (projected, input_grad, weight_grad)


def solution(mesh):
    in_specs = (P("fsdp", "node"), P("fsdp", "node"), P("fsdp", "node"))
    out_specs = (P("fsdp", "node"), P("fsdp", "node"), P("fsdp", "node"))
    return jax.shard_map(body, mesh=mesh, in_specs=in_specs, out_specs=out_specs, check_vma=False)
```

profile of v0, /device:TPU:1, one launch (start us, length us, event | category | flops | bytes accessed | tf_op | source)
XLA Modules:
  0.0 403.2 jit_solution(3688470017451927738)
XLA Ops:
  7.2 0.0 copy-start
  7.2 0.0 all-gather.3.cloned.1.call-start
  7.2 0.7 all-gather.3.cloned.1.call-update
  7.9 0.0 all-gather.5.cloned.1.call-start
  8.0 0.7 all-gather.5.cloned.1.call-update
  8.7 0.0 reduce-scatter.5.cloned.1.call-start
  8.7 96.3 %all-gather.3.cloned.1.call-done = bf16[512,8192]{1,0:T(8,128)(2,1)} async-done(((bf16[512,1024]{1,0:T(8,128)(2,1)}), bf16[512,8192]{1,0:T(8,128)(2,1)}) %all-gather.3.cloned.1.call-update) | async-done | bytes 8388624 | tf_op jit(solution)/shard_map/all_gather | solution.py:8
  105.0 0.0 copy-done
  105.0 11.4 %convolution_convert_fusion = bf16[8192,640]{1,0:T(8,128)(2,1)} fusion(bf16[512,8192]{1,0:T(8,128)(2,1)} %all-gather.3.cloned.1.call-done, bf16[512,640]{1,0:T(8,128)(2,1)S(1)} %copy-done), kind=kOutput, calls=%fused_computation | convolution fusion | flops 5373952000 | bytes 19529728 | tf_op jit(solution)/shard_map/dot_general | solution.py:27
  116.4 0.0 reduce-scatter.5.cloned.1.call-update
  116.5 0.0 reduce-scatter.3.cloned.1.call-start
  116.5 71.4 %all-gather.5.cloned.1.call-done = bf16[8192,640]{1,0:T(8,128)(2,1)} async-done(((bf16[512,640]{1,0:T(8,128)(2,1)}), bf16[8192,640]{1,0:T(8,128)(2,1)}) %all-gather.5.cloned.1.call-update) | async-done | bytes 10485776 | tf_op jit(solution)/shard_map/all_gather | solution.py:12
  188.0 13.0 %convolution_convert_fusion.1 = bf16[512,8192]{1,0:T(8,128)(2,1)} fusion(bf16[512,640]{1,0:T(8,128)(2,1)S(1)} %copy-done, bf16[8192,640]{1,0:T(8,128)(2,1)} %all-gather.5.cloned.1.call-done), kind=kOutput, calls=%fused_computation.1 | convolution fusion | flops 5372903424 | bytes 19529728 | tf_op jit(solution)/shard_map/dot_general | solution.py:15
  200.9 0.0 reduce-scatter.3.cloned.1.call-update
  200.9 14.5 %convolution_convert_fusion.2 = bf16[512,640]{1,0:T(8,128)(2,1)} fusion(bf16[512,8192]{1,0:T(8,128)(2,1)} %all-gather.3.cloned.1.call-done, bf16[8192,640]{1,0:T(8,128)(2,1)} %all-gather.5.cloned.1.call-done), kind=kOutput, calls=%fused_computation.2 | convolution fusion | flops 5369036800 | bytes 19529728 | tf_op jit(solution)/shard_map/dot_general | solution.py:10
  215.5 85.6 %reduce-scatter.5.cloned.1.call-done = bf16[512,640]{1,0:T(8,128)(2,1)} async-done(((bf16[8192,640]{1,0:T(8,128)(2,1)}), bf16[512,640]{1,0:T(8,128)(2,1)}) %reduce-scatter.5.cloned.1.call-update) | async-done | bytes 655376 | tf_op jit(solution)/shard_map/reduce_scatter | solution.py:26
  301.1 2.2 convert_element_type.15
  303.3 93.3 %reduce-scatter.3.cloned.1.call-done = bf16[512,1024]{1,0:T(8,128)(2,1)} async-done(((bf16[512,8192]{1,0:T(8,128)(2,1)}), bf16[512,1024]{1,0:T(8,128)(2,1)}) %reduce-scatter.3.cloned.1.call-update) | async-done | bytes 1048592 | tf_op jit(solution)/shard_map/reduce_scatter | solution.py:22
Async XLA Ops:
  7.2 97.8 %copy-start = (bf16[512,640]{1,0:T(8,128)(2,1)S(1)}, bf16[512,640]{1,0:T(8,128)(2,1)}, u32[]{:S(2)}) copy-start(bf16[512,640]{1,0:T(8,128)(2,1)} %param.5) | copy-start | bytes 1966084
  7.2 97.8 %all-gather.3.cloned.1.call-start = ((), (), s32[]{:S(2)}) async-start(), calls=%async_computation.2 | async-start | bytes 9437184 | tf_op jit(solution)/shard_map/all_gather | solution.py:8
  7.9 180.0 %all-gather.5.cloned.1.call-start = ((), (), s32[]{:S(2)}) async-start(), calls=%async_computation.3 | async-start | bytes 11141120 | tf_op jit(solution)/shard_map/all_gather | solution.py:12
  8.7 292.4 %reduce-scatter.5.cloned.1.call-start = ((), (), s32[]{:S(2)}) async-start(), calls=%async_computation.5 | async-start | bytes 11141120 | tf_op jit(solution)/shard_map/reduce_scatter | solution.py:26
  116.5 280.2 %reduce-scatter.3.cloned.1.call-start = ((), (), s32[]{:S(2)}) async-start(), calls=%async_computation.4 | async-start | bytes 9437184 | tf_op jit(solution)/shard_map/reduce_scatter | solution.py:22
Sparse Core Ops, SparseCore 0:
  9.7 95.2 all-gather.2
  107.4 80.5 all-gather.4
  192.3 108.7 reduce-scatter.4
  304.1 92.5 reduce-scatter.2
where the time goes:
time: 403 us
  waiting for transfers between devices  348 us (86%)
  matrix products  38.9 us (10%)
  between operations  13.8 us (3%)
    all_gather x1, waiting for transfers between devices, body(): gathered = lax.all_gather(activations, 'node', axis=1, tiled=True)  96.3 us
    reduce_scatter x1, waiting for transfers between devices, body(): lax.psum_scatter(partial_sum.astype(jnp.bfloat16), 'node', scatter_dimens...  93.3 us
    reduce_scatter x1, waiting for transfers between devices, body(): lax.psum_scatter(lax.dot_general(feature_cols, qkv_grad, (((0,), (0,)), (...  85.6 us
    all_gather x1, waiting for transfers between devices, body(): lax.all_gather(qkv_weight, 'fsdp', axis=0, tiled=True)  71.4 us
    dot_general x1, matrix products, body(): jnp.dot(feature_cols, lax.all_gather(qkv_weight, 'fsdp', axis=0, tiled=Tr...  14.5 us
    dot_general x1, matrix products, body(): lax.dot_general(qkv_grad, lax.all_gather(qkv_weight, 'fsdp', axis=0, tile...  13 us
    dot_general x1, matrix products, body(): lax.dot_general(feature_cols, qkv_grad, (((0,), (0,)), ((), ())), preferr...  11.4 us
  transfers between devices with their start and end apart: 4, of which 4 were waited for; matrix products, arithmetic and copies ran while one was open for 10% of the time, Pallas kernels for 0%

commit v1 on v0

--- a/solution.py
+++ b/solution.py
@@ -5,7 +5,9 @@
 
 
 def body(activations, qkv_weight, qkv_grad):
-    gathered = lax.all_gather(activations, "node", axis=1, tiled=True)
+    gathered = jnp.concatenate(
+        lax.all_to_all(jnp.stack([activations] * lax.axis_size("node")), "node", 0, 0), axis=1
+    )
     feature_cols = gathered
     forward = jnp.dot(
         feature_cols,

time: 403 us -> 372 us (0.923)
  waiting for transfers between devices: 348 us -> 179 us
  blocking collectives: 0 us -> 135 us
  local copies, waits for them, and re-layouts: 0.01 us -> 5.49 us
    all_to_all x0 -> x1, blocking collectives: none -> 135 us  [body(): lax.all_to_all(jnp.stack([activations] * lax.axis_size('node')), 'node',...]
    all_gather x1 -> x0, waiting for transfers between devices: 96.3 us -> none  [body(): gathered = lax.all_gather(activations, 'node', axis=1, tiled=True)]
    all_gather x1, waiting for transfers between devices: 71.4 us -> 0.02 us  [body(): lax.all_gather(qkv_weight, 'fsdp', axis=0, tiled=True)]
    unnamed x2 -> x5, local copies, waits for them, and re-layouts: 0.01 us -> 4.77 us
  transfers between devices with their start and end apart: 4 -> 3, of which waited for: 4 -> 2; matrix products, arithmetic and copies ran while one was open for 10% -> 11% of each run, Pallas kernels for 0% -> 0%
where the time goes in v1:
time: 372 us
  waiting for transfers between devices  179 us (48%)
  blocking collectives  135 us (36%)
  matrix products  36.7 us (10%)
  between operations  13.8 us (4%)
  local copies, waits for them, and re-layouts  5.49 us (1%)
    all_to_all x1, blocking collectives, body(): lax.all_to_all(jnp.stack([activations] * lax.axis_size('node')), 'node',...  135 us
    reduce_scatter x1, waiting for transfers between devices, body(): lax.psum_scatter(partial_sum.astype(jnp.bfloat16), 'node', scatter_dimens...  93.5 us
    reduce_scatter x1, waiting for transfers between devices, body(): lax.psum_scatter(lax.dot_general(feature_cols, qkv_grad, (((0,), (0,)), (...  84.5 us
    dot_general x1, matrix products, body(): jnp.dot(feature_cols, lax.all_gather(qkv_weight, 'fsdp', axis=0, tiled=Tr...  14.6 us
    dot_general x1, matrix products, body(): lax.dot_general(qkv_grad, lax.all_gather(qkv_weight, 'fsdp', axis=0, tile...  13 us
    dot_general x1, matrix products, body(): lax.dot_general(feature_cols, qkv_grad, (((0,), (0,)), ((), ())), preferr...  9.13 us
  transfers between devices with their start and end apart: 3, of which 2 were waited for; matrix products, arithmetic and copies ran while one was open for 11% of the time, Pallas kernels for 0%

profile of v1, /device:TPU:1, one launch (start us, length us, event | category | flops | bytes accessed | tf_op | source)
XLA Modules:
  0.0 371.9 jit_solution(7724117516742864224)
XLA Ops:
  7.2 0.0 copy-start
  7.2 0.0 all-gather.2.cloned.1.call-start
  7.2 0.7 all-gather.2.cloned.1.call-update
  7.9 0.0 reduce-scatter.5.cloned.1.call-start
  8.0 1.5 copy.6
  9.5 0.7 stack.2
  10.2 134.9 %all_to_all.5 = bf16[8,512,1024]{1,2,0:T(8,128)(2,1)S(1)} all-to-all(bf16[8,512,1024]{1,2,0:T(8,128)(2,1)S(1)} %stack.2), channel_id=1, replica_groups=mesh['fsdp'=16,'node'=8] {'node'}, dimensions={0} | all-to-all | bytes 16777216 | tf_op jit(solution)/shard_map/all_to_all | solution.py:9
  145.1 0.0 copy-start.1
  145.1 3.3 copy-done.1
  148.3 0.0 copy-done
  148.3 9.1 %convolution_convert_fusion = bf16[8192,640]{1,0:T(8,128)(2,1)} fusion(bf16[512,8192]{0,1:T(8,128)(2,1)S(1)} %bitcast.9, bf16[512,640]{1,0:T(8,128)(2,1)S(1)} %copy-done), kind=kOutput, calls=%fused_computation | convolution fusion | flops 5373952000 | bytes 19529728 | tf_op jit(solution)/shard_map/dot_general | solution.py:29
  157.5 0.0 reduce-scatter.5.cloned.1.call-update
  157.5 0.0 reduce-scatter.3.cloned.1.call-start
  157.5 0.0 all-gather.2.cloned.1.call-done
  157.6 13.0 %convolution_convert_fusion.1 = bf16[512,8192]{1,0:T(8,128)(2,1)} fusion(bf16[512,640]{1,0:T(8,128)(2,1)S(1)} %copy-done, bf16[8192,640]{1,0:T(8,128)(2,1)} %all-gather.2.cloned.1.call-done), kind=kOutput, calls=%fused_computation.1 | convolution fusion | flops 5372903424 | bytes 19529728 | tf_op jit(solution)/shard_map/dot_general | solution.py:17
  170.5 0.0 reduce-scatter.3.cloned.1.call-update
  170.6 14.6 %convolution_convert_fusion.2 = bf16[512,640]{1,0:T(8,128)(2,1)} fusion(bf16[512,8192]{0,1:T(8,128)(2,1)} %bitcast.10, bf16[8192,640]{1,0:T(8,128)(2,1)} %all-gather.2.cloned.1.call-done), kind=kOutput, calls=%fused_computation.2 | convolution fusion | flops 5369036800 | bytes 19529728 | tf_op jit(solution)/shard_map/dot_general | solution.py:12
  185.2 84.5 %reduce-scatter.5.cloned.1.call-done = bf16[512,640]{1,0:T(8,128)(2,1)} async-done(((bf16[8192,640]{1,0:T(8,128)(2,1)}), bf16[512,640]{1,0:T(8,128)(2,1)}) %reduce-scatter.5.cloned.1.call-update) | async-done | bytes 655376 | tf_op jit(solution)/shard_map/reduce_scatter | solution.py:28
  269.7 2.2 convert_element_type.15
  271.9 93.5 %reduce-scatter.3.cloned.1.call-done = bf16[512,1024]{1,0:T(8,128)(2,1)} async-done(((bf16[512,8192]{1,0:T(8,128)(2,1)}), bf16[512,1024]{1,0:T(8,128)(2,1)}) %reduce-scatter.3.cloned.1.call-update) | async-done | bytes 1048592 | tf_op jit(solution)/shard_map/reduce_scatter | solution.py:24
Async XLA Ops:
  7.2 141.2 %copy-start = (bf16[512,640]{1,0:T(8,128)(2,1)S(1)}, bf16[512,640]{1,0:T(8,128)(2,1)}, u32[]{:S(2)}) copy-start(bf16[512,640]{1,0:T(8,128)(2,1)} %param.5) | copy-start | bytes 1966084
  7.2 150.4 %all-gather.2.cloned.1.call-start = ((), (), s32[]{:S(2)}) async-start(), calls=%async_computation.3 | async-start | bytes 11141120 | tf_op jit(solution)/shard_map/all_gather | solution.py:14
  7.9 261.8 %reduce-scatter.5.cloned.1.call-start = ((), (), s32[]{:S(2)}) async-start(), calls=%async_computation.5 | async-start | bytes 11141120 | tf_op jit(solution)/shard_map/reduce_scatter | solution.py:28
  145.1 3.3 copy-start.1
  157.5 207.9 %reduce-scatter.3.cloned.1.call-start = ((), (), s32[]{:S(2)}) async-start(), calls=%async_computation.4 | async-start | bytes 9437184 | tf_op jit(solution)/shard_map/reduce_scatter | solution.py:24
Sparse Core Ops, SparseCore 0:
  10.4 120.6 all-gather.1
  157.6 112.0 reduce-scatter.4
  272.8 92.5 reduce-scatter.2
